TPU v7x, 32 devices: a whole 2x2x4 slice. The times are simulated.
32 devices in a mesh: leaf: 2 (over y), grow: 4 (over z), gcol: 4 (over x, core).
Axes of the slice: x: 2, y: 2, z: 4, core: 2. Of those that a mesh axis runs over, the one named last changes fastest.
Arguments:
- right_leaf: float32 [2, 4, 4, 512, 256], P('leaf', 'grow', 'gcol'), may hold values from -6 to 6
- inverse_leaf: float32 [2, 4, 4, 512, 512], P('leaf', 'grow', 'gcol'), may hold values from -2 to 2
- lower_leaf: float32 [2, 4, 4, 512, 512], P('leaf', 'grow', 'gcol'), may hold values from -0.25 to 0.25
- present: int32 [2, 4, 4], P('leaf', 'grow', 'gcol'), may hold values 0 or 1
- right_middle: float32 [2, 4, 512, 256], P('leaf', 'grow', 'gcol'), may hold values from -6 to 6
- inverse_middle: float32 [2, 4, 512, 512], P('leaf', 'grow', 'gcol'), may hold values from -2 to 2
- upper_middle: float32 [2, 2, 4, 512, 512], P(None, 'leaf', 'grow', 'gcol'), may hold values from -0.09375 to 0.09375
- right_top: float32 [2, 512, 256], P(None, 'gcol'), may hold values from -6 to 6
- inverse_top: float32 [2, 512, 512], P(None, 'gcol'), may hold values from -2 to 2
- upper_top: float32 [1, 512, 512], P(None, 'gcol'), may hold values from -0.25 to 0.25
Outputs:
- solve_leaf: float32 [2, 4, 4, 512, 256], P('leaf', 'grow', 'gcol')
- solve_middle: float32 [2, 4, 512, 256], P('leaf', 'grow', 'gcol')
- solve_top: float32 [2, 512, 256], P(None, 'gcol')
All inputs are finite; a program needn't handle non-finite values. No bound on the sum of `present` on one device may be relied on, other than what follows from the above.
Results may differ from a plain program's by a relative error of at most 0.00016.
Values sent between devices are 32-bit elements; how exact they have to be, the bound alone decides.
A program may use at most 64 MiB of HBM per device.

v0:
```python
import jax
import jax.numpy as jnp
from jax import lax
from jax.sharding import PartitionSpec as P

PRECISE = lax.Precision.HIGHEST


def from_partner(value, axis, apart):
    mask = 2**apart
    pairs = [(source, source ^ mask) for source in range(lax.axis_size(axis))]
    return lax.ppermute(value, axis, pairs)


def product(factor, vector):
    return jnp.dot(factor, vector, precision=PRECISE, preferred_element_type=jnp.float32)


def transposed_product(factor, vector):
    return lax.dot_general(
        factor,
        vector,
        (((0,), (0,)), ((), ())),
        precision=PRECISE,
        preferred_element_type=jnp.float32,
    )


def pair_index(upper_level, lower_level):
    return upper_level * (upper_level - 1) // 2 + lower_level


def widen(fragment, row_start, full_rows):
    blank = jnp.zeros((full_rows, fragment.shape[1]), jnp.float32)
    return lax.dynamic_update_slice_in_dim(blank, fragment, row_start, 0)


def combine_layers(stacked, row_keep):
    stacked = lax.psum(stacked * row_keep, ("grow", "gcol"))
    for which_bit in range(lax.axis_size("leaf").bit_length() - 1):
        partner = from_partner(stacked, "leaf", which_bit)
        stacked = stacked + partner
    return stacked


def local(
    right_leaf,
    inverse_leaf,
    lower_leaf,
    present,
    right_middle,
    inverse_middle,
    upper_middle,
    right_top,
    inverse_top,
    upper_top,
):
    levels_count = right_top.shape[0]
    block_size = inverse_leaf.shape[-1]
    share_rows = inverse_middle.shape[2]
    row_start = lax.axis_index("gcol") * share_rows
    row_keep = jnp.ones((1, 1, 1), jnp.float32)
    kept_block = present[0, 0, 0].astype(jnp.float32)
    leaf_fwd = product(inverse_leaf[0, 0, 0], right_leaf[0, 0, 0])
    middle_part = product(lower_leaf[0, 0, 0], leaf_fwd * kept_block) - widen(
        right_middle[0, 0], row_start, block_size
    )
    middle_total = lax.psum(middle_part, "gcol")
    middle_fwd = product(inverse_middle[0, 0], -middle_total)
    lead_device = jnp.where(
        (lax.axis_index("leaf") == 0) & (lax.axis_index("grow") == 0), 1.0, 0.0
    ).astype(jnp.float32)
    top_rights = [widen(right_top[height], row_start, block_size) for height in range(levels_count)]
    partials = [
        transposed_product(upper_middle[height, 0, 0], middle_fwd)
        - lead_device * top_rights[height]
        for height in range(levels_count)
    ]
    top_fwd = []
    totals = combine_layers(jnp.stack(partials), row_keep)
    for upper_level in range(levels_count):
        residual = -totals[upper_level]
        if upper_level > 0:
            link_terms = transposed_product(upper_top[pair_index(upper_level, 0)], top_fwd[0])
            residual = residual - lax.psum(link_terms, "gcol")
        top_fwd.append(product(inverse_top[upper_level], residual))
    top_back = [None] * levels_count
    for upper_level in reversed(range(levels_count)):
        residual = top_fwd[upper_level]
        for higher_level in range(upper_level + 1, levels_count):
            residual = residual - product(
                upper_top[pair_index(higher_level, upper_level)], top_back[higher_level]
            )
        top_piece = transposed_product(inverse_top[upper_level], residual)
        top_back[upper_level] = lax.psum(top_piece, "gcol")
    middle_res = middle_fwd
    for height in range(levels_count):
        middle_res = middle_res - product(upper_middle[height, 0, 0], top_back[height])
    middle_piece = transposed_product(inverse_middle[0, 0], middle_res)
    middle_back = lax.psum(middle_piece, "gcol")
    leaf_res = leaf_fwd - transposed_product(lower_leaf[0, 0, 0], middle_back) * kept_block
    leaf_back = transposed_product(inverse_leaf[0, 0, 0], leaf_res)
    solve_middle = lax.dynamic_slice_in_dim(middle_back, row_start, share_rows, 0)
    solve_top = jnp.stack(
        [lax.dynamic_slice_in_dim(top_whole, row_start, share_rows, 0) for top_whole in top_back]
    )
    return (leaf_back[None, None, None], solve_middle[None, None], solve_top)


def solution(mesh):
    in_specs = (
        P("leaf", "grow", "gcol", None, None),
        P("leaf", "grow", "gcol", None, None),
        P("leaf", "grow", "gcol", None, None),
        P("leaf", "grow", "gcol"),
        P("leaf", "grow", "gcol", None),
        P("leaf", "grow", "gcol", None),
        P(None, "leaf", "grow", "gcol", None),
        P(None, "gcol", None),
        P(None, "gcol", None),
        P(None, "gcol", None),
    )
    out_specs = (
        P("leaf", "grow", "gcol", None, None),
        P("leaf", "grow", "gcol", None),
        P(None, "gcol", None),
    )
    return jax.shard_map(local, mesh=mesh, in_specs=in_specs, out_specs=out_specs, check_vma=False)
```

profile of v0, /device:TPU:0, one launch (start us, length us, event | category | flops | bytes accessed | tf_op | source)
XLA Modules:
  0.0 332.5 jit_solution(13451472588966247061)
XLA Ops:
  8.0 1.0 copy.17
  9.0 2.3 fusion.10
  11.4 2.7 fusion.2
  15.4 34.7 %all-reduce.7.cloned.1.call-done = f32[512,256]{0,1:T(8,128)} async-done(((f32[512,256]{0,1:T(8,128)}), f32[512,256]{0,1:T(8,128)}) %all-reduce.7.cloned.1.call-update) | async-done | bytes 524304 | tf_op jit(solution)/shard_map/psum | solution.py:68
  50.2 1.6 fusion.20
  53.0 1.1 pad_maximum_fusion
  54.1 93.4 %all-reduce.9.cloned.1.call-done = f32[2,512,256]{1,2,0:T(8,128)} async-done(((f32[2,512,256]{1,2,0:T(8,128)}), f32[2,512,256]{1,2,0:T(8,128)}) %all-reduce.9.cloned.1.call-update) | async-done | bytes 1048592 | tf_op jit(solution)/shard_map/psum | solution.py:39
  147.5 1.5 collective-permute-start
  149.0 23.0 %collective-permute-done = f32[2,512,256]{1,2,0:T(8,128)S(1)} collective-permute-done((f32[2,512,256]{1,2,0:T(8,128)}, f32[2,512,256]{1,2,0:T(8,128)S(1)}, u32[]{:S(2)}, u32[]{:S(2)}) %collective-permute-start) | collective-permute-done | bytes 1048608 | tf_op jit(solution)/shard_map/ppermute | solution.py:12
  172.0 1.4 add.17
  174.4 1.4 convolution_bitcast_fusion.4
  175.8 32.3 %all-reduce.11.cloned.1.call-done = f32[512,256]{0,1:T(8,128)} async-done(((f32[512,256]{0,1:T(8,128)}), f32[512,256]{0,1:T(8,128)}) %all-reduce.11.cloned.1.call-update) | async-done | bytes 524304 | tf_op jit(solution)/shard_map/psum | solution.py:85
  208.1 1.6 fusion.14
  209.8 1.4 convolution_bitcast_fusion.3
  211.2 33.3 %all-reduce.13.cloned.1.call-done = f32[512,256]{0,1:T(8,128)} async-done(((f32[512,256]{0,1:T(8,128)}), f32[512,256]{0,1:T(8,128)}) %all-reduce.13.cloned.1.call-update) | async-done | bytes 524304 | tf_op jit(solution)/shard_map/psum | solution.py:95
  244.5 1.6 convolution_subtract_fusion.2
  246.1 1.4 convolution_bitcast_fusion.2
  247.8 33.1 %all-reduce.15.cloned.1.call-done = f32[512,256]{0,1:T(8,128)} async-done(((f32[512,256]{0,1:T(8,128)}), f32[512,256]{0,1:T(8,128)}) %all-reduce.15.cloned.1.call-update) | async-done | bytes 524304 | tf_op jit(solution)/shard_map/psum | solution.py:95
  280.9 1.6 convolution_subtract_fusion.1
  283.4 1.4 convolution_bitcast_fusion.1
  285.0 33.2 %all-reduce.17.cloned.1.call-done = f32[512,256]{0,1:T(8,128)} async-done(((f32[512,256]{0,1:T(8,128)}), f32[512,256]{0,1:T(8,128)}) %all-reduce.17.cloned.1.call-update) | async-done | bytes 524304 | tf_op jit(solution)/shard_map/psum | solution.py:100
  318.2 2.8 fusion.1
  321.0 1.1 convolution_bitcast_fusion
  322.1 1.0 copy.23
  (53 shorter events, 7.6 us)
Async XLA Ops:
  7.2 4.2 %copy-start = (f32[1,1,1,512,512]{4,3,2,1,0:T(8,128)S(1)}, f32[1,1,1,512,512]{4,3,2,1,0:T(8,128)}, u32[]{:S(2)}) copy-start(f32[1,1,1,512,512]{4,3,2,1,0:T(8,128)} %param.12) | copy-start | bytes 3145732
  7.2 43.0 %all-reduce.7.cloned.1.call-start = ((), (), s32[]{:S(2)}) async-start(), calls=%async_computation | async-start | bytes 1048576 | tf_op jit(solution)/shard_map/psum | solution.py:68
  14.1 0.9 copy-start.10
  14.1 133.4 %all-reduce.9.cloned.1.call-start = ((), (), s32[]{:S(2)}) async-start(), calls=%async_computation.1 | async-start | bytes 2097152 | tf_op jit(solution)/shard_map/psum | solution.py:39
  15.4 34.8 %copy-start.6 = (f32[1,1,128,512]{3,2,1,0:T(8,128)S(1)}, f32[1,1,128,512]{3,2,1,0:T(8,128)}, u32[]{:S(2)}) copy-start(f32[1,1,128,512]{3,2,1,0:T(8,128)} %param.15) | copy-start | bytes 786436
  15.4 36.4 %copy-start.4 = (f32[2,1,1,128,512]{4,3,2,1,0:T(8,128)S(1)}, f32[2,1,1,128,512]{4,3,2,1,0:T(8,128)}, u32[]{:S(2)}) copy-start(f32[2,1,1,128,512]{4,3,2,1,0:T(8,128)} %param.16) | copy-start | bytes 1572868
  54.0 119.4 %copy-start.3 = (f32[2,128,512]{2,1,0:T(8,128)S(1)}, f32[2,128,512]{2,1,0:T(8,128)}, u32[]{:S(2)}) copy-start(f32[2,128,512]{2,1,0:T(8,128)} %param.18) | copy-start | bytes 1572868
  54.1 154.1 %all-reduce.11.cloned.1.call-start = ((), (), s32[]{:S(2)}) async-start(), calls=%async_computation.2 | async-start | bytes 1048576 | tf_op jit(solution)/shard_map/psum | solution.py:85
  147.5 24.5 %collective-permute-start = (f32[2,512,256]{1,2,0:T(8,128)}, f32[2,512,256]{1,2,0:T(8,128)S(1)}, u32[]{:S(2)}, u32[]{:S(2)}) collective-permute-start(f32[2,512,256]{1,2,0:T(8,128)} %all-reduce.9.cloned.1.call-done), channel_id=1, source_target_pairs={{0,16},{16,0},{1,17},{17,1},{2,18},{18,2},{3,19},{19,3},{4,20},{20... | collective-permute-start | bytes 3145736 | tf_op jit(solution)/shard_map/ppermute | solution.py:12
  173.4 1.0 copy-start.8
  175.8 68.7 %all-reduce.13.cloned.1.call-start = ((), (), s32[]{:S(2)}) async-start(), calls=%async_computation.3 | async-start | bytes 1048576 | tf_op jit(solution)/shard_map/psum | solution.py:95
  211.1 33.4 %copy-start.9 = (f32[1,128,512]{2,1,0:T(8,128)S(1)}, f32[1,128,512]{2,1,0:T(8,128)}, u32[]{:S(2)}) copy-start(f32[1,128,512]{2,1,0:T(8,128)} %param.19) | copy-start | bytes 786436
  211.2 69.7 %all-reduce.15.cloned.1.call-start = ((), (), s32[]{:S(2)}) async-start(), calls=%async_computation.4 | async-start | bytes 1048576 | tf_op jit(solution)/shard_map/psum | solution.py:95
  246.1 34.7 %copy-start.5 = (f32[2,1,1,128,512]{4,3,2,1,0:T(8,128)S(1)}, f32[2,1,1,128,512]{4,3,2,1,0:T(8,128)}, u32[]{:S(2)}) copy-start(f32[2,1,1,128,512]{4,3,2,1,0:T(8,128)} %param.16) | copy-start | bytes 1572868
  247.5 35.0 %copy-start.2 = (f32[512,256]{0,1:T(8,128)S(1)}, f32[512,256]{0,1:T(8,128)}, u32[]{:S(2)}) copy-start(f32[512,256]{0,1:T(8,128)} %all-reduce.13.cloned.1.call-done) | copy-start | bytes 1572868
  247.5 70.6 %all-reduce.17.cloned.1.call-start = ((), (), s32[]{:S(2)}) async-start(), calls=%async_computation.5 | async-start | bytes 1048576 | tf_op jit(solution)/shard_map/psum | solution.py:100
  282.5 1.0 copy-start.7
  285.0 36.1 %copy-start.1 = (f32[1,1,1,512,512]{4,3,2,1,0:T(8,128)S(1)}, f32[1,1,1,512,512]{4,3,2,1,0:T(8,128)}, u32[]{:S(2)}) copy-start(f32[1,1,1,512,512]{4,3,2,1,0:T(8,128)} %param.11) | copy-start | bytes 3145732
Sparse Core Ops, SparseCore 0:
  14.2 35.8 all-reduce.6
  54.2 93.2 all-reduce.8
  175.9 32.1 all-reduce.10
  211.3 33.1 all-reduce.12
  247.6 33.1 all-reduce.14
  285.0 33.1 all-reduce.16
where the time goes:
time: 333 us
  waiting for transfers between devices  283 us (85%)
  matrix products  23.2 us (7%)
  between operations  15.2 us (5%)
  local copies, waits for them, and re-layouts  5.98 us (2%)
    psum x1, waiting for transfers between devices, combine_layers(): stacked = lax.psum(stacked * row_keep, ('grow', 'gcol'))  93.4 us
    psum x2, waiting for transfers between devices, local(): top_back[upper_level] = lax.psum(top_piece, 'gcol')  66.4 us
    psum x1, waiting for transfers between devices, local(): middle_total = lax.psum(middle_part, 'gcol')  34.7 us
    psum x1, waiting for transfers between devices, local(): middle_back = lax.psum(middle_piece, 'gcol')  33.2 us
    psum x1, waiting for transfers between devices, local(): residual = residual - lax.psum(link_terms, 'gcol')  32.3 us
    ppermute x1, waiting for transfers between devices, from_partner(): return lax.ppermute(value, axis, pairs)  23 us
    dot_general x8, matrix products, product(): jnp.dot(factor, vector, precision=PRECISE, preferred_element_type=jnp.flo...  12.7 us
    dot_general x8, matrix products, transposed_product(): lax.dot_general(factor, vector, (((0,), (0,)), ((), ())), precision=PRECI...  10.5 us
  transfers between devices with their start and end apart: 7, of which 7 were waited for; matrix products, arithmetic and copies ran while one was open for 0% of the time, Pallas kernels for 0%

commit v1 on v0

v1 whole, which is shorter than its diff:
```python
import functools

import jax
import jax.numpy as jnp
from jax import lax
from jax.experimental import pallas as pl
from jax.experimental.pallas import tpu as pltpu
from jax.sharding import PartitionSpec as P

AXES = ("gcol", "leaf", "grow")
NN = ((1,), (0,))
NT = ((1,), (1,))


def pair_index(upper_level, lower_level):
    return upper_level * (upper_level - 1) // 2 + lower_level


def split(value):
    high = value.astype(jnp.bfloat16)
    low = (value - high.astype(jnp.float32)).astype(jnp.bfloat16)
    return high, low


def mul(left, right, dims=NN):
    def dot(a, b):
        return lax.dot_general(a, b, (dims, ((), ())), preferred_element_type=jnp.float32)

    return dot(left[0], right[0]) + (dot(left[0], right[1]) + dot(left[1], right[0]))


class Plan:
    def __init__(self, sizes, levels, block, columns):
        self.sizes, self.levels, self.block, self.columns = sizes, levels, block, columns
        self.n = sizes["gcol"]
        self.gbits = [("gcol", t) for t in range(self.n.bit_length() - 1)]
        others = [(a, t) for a in AXES[1:] for t in range(sizes[a].bit_length() - 1)]
        bits = self.gbits + others
        count = 0
        while count < len(bits) and columns >> (count + 1) >= 8:
            count += 1
        count = max(count, len(self.gbits))
        self.halved, self.rest = bits[:count], bits[count:]
        self.chunk = columns >> count
        first = self.gbits[:1]
        self.orders = [
            self.halved,
            first
            + [b for b in self.halved if b[0] == "leaf"]
            + [b for b in self.halved if b[0] == "gcol" and b not in first]
            + [b for b in self.halved if b[0] == "grow"],
        ]
        self.all_bits = bits

    def order(self, level):
        return self.orders[level % 2]


def kernel(
    plan,
    right_leaf,
    inverse_leaf,
    lower_leaf,
    present,
    right_middle,
    inverse_middle,
    upper_middle,
    right_top,
    inverse_top,
    upper_top,
    solve_leaf,
    solve_middle,
    solve_top,
    *scratch,
):
    names = [name for name, _ in scratch_list(plan)]
    s = dict(zip(names, scratch))
    send, recv = s["send"], s["recv"]
    n, levels, block, columns, chunk = plan.n, plan.levels, plan.block, plan.columns, plan.chunk
    share = block // n
    nbits = len(plan.gbits)
    place = {axis: lax.axis_index(axis) for axis in AXES}
    me = place["gcol"]
    counter = [0]

    def bit_of(bit):
        return (place[bit[0]] // 2 ** bit[1]) % 2

    def partner(bit):
        return {bit[0]: place[bit[0]] + (1 - 2 * bit_of(bit)) * 2 ** bit[1]}

    def ship(source, target, bit):
        slot = counter[0]
        counter[0] += 1
        copy = pltpu.make_async_remote_copy(
            src_ref=source,
            dst_ref=target,
            send_sem=send.at[slot],
            recv_sem=recv.at[slot],
            device_id=partner(bit),
            device_id_type=pl.DeviceIdType.MESH,
        )
        copy.start()
        return copy

    barrier = pltpu.get_barrier_semaphore()
    for bit in plan.all_bits:
        pl.semaphore_signal(
            barrier, inc=1, device_id=partner(bit), device_id_type=pl.DeviceIdType.MESH
        )

    kept = present[0, 0, 0].astype(jnp.float32)
    leaf_fwd = mul(split(inverse_leaf[0, 0, 0]), split(right_leaf[0, 0, 0]))
    s["leaf_fwd"][...] = leaf_fwd
    part = mul(split(lower_leaf[0, 0, 0]), split(leaf_fwd)) * kept
    s["mid"][...] = part.reshape(n, share, columns)
    pl.semaphore_wait(barrier, len(plan.all_bits))

    def scatter_sum(blocks, landing, idle=None):
        at = 0
        for t, bit in enumerate(plan.gbits):
            low = me % 2**t
            count = n >> (t + 1)
            theirs = low + (1 - bit_of(bit)) * 2**t
            mine = low + bit_of(bit) * 2**t
            copies = [
                ship(blocks.at[theirs + j * 2 ** (t + 1)], landing.at[at + j], bit)
                for j in range(count)
            ]
            if idle is not None:
                idle(t)
            for j, copy in enumerate(copies):
                copy.wait()
                where = mine + j * 2 ** (t + 1)
                blocks[where] = blocks[where] + landing[at + j]
            at += count

    def gather(blocks, idle=None):
        for t in reversed(range(nbits)):
            low = me % 2 ** (t + 1)
            copies = [
                ship(*(blocks.at[low + j * 2 ** (t + 1)],) * 2, plan.gbits[t])
                for j in range(n >> (t + 1))
            ]
            if idle is not None:
                idle(t)
            for copy in copies:
                copy.wait()

    def fill_transposes(t):
        if t == nbits - 1:
            high, low = split(inverse_leaf[0, 0, 0].T)
            s["inv_high"][...] = high
            s["inv_low"][...] = low

    def fill_lower(t):
        if t == nbits - 1:
            high, low = split(lower_leaf[0, 0, 0].T)
            s["low_high"][...] = high
            s["low_low"][...] = low

    scatter_sum(s["mid"], s["mid_land"], fill_transposes)
    s["mid_full"][me] = right_middle[0, 0] - s["mid"][me]
    gather(s["mid_full"], fill_lower)
    inv_mid = inverse_middle[0, 0]
    middle_fwd = mul(split(inv_mid), split(s["mid_full"][...].reshape(block, columns)))

    lead = ((place["leaf"] + place["grow"]) == 0).astype(jnp.float32)
    fwd_turned = split(middle_fwd.T)
    bits_shape = (2,) * len(plan.halved)
    for level in range(levels):
        turned = mul(fwd_turned, split(upper_middle[level, 0, 0]))
        right = right_top[level].T * lead
        placed = jnp.concatenate(
            [right * (me == c).astype(jnp.float32) for c in range(n)], axis=1
        )
        s[f"top{level}"][...] = (placed - turned).reshape(bits_shape + (chunk, block))

    def index(done, bit=None, flip=False):
        where = []
        for b in plan.halved:
            if b in done:
                where.append(bit_of(b))
            elif b == bit:
                where.append(1 - bit_of(b) if flip else bit_of(b))
            else:
                where.append(slice(None))
        return tuple(where)

    for step in range(len(plan.halved)):
        copies = []
        for level in range(levels):
            order = plan.order(level)
            top = s[f"top{level}"]
            there = index(order[:step], order[step], True)
            copies.append(ship(top.at[there], s[f"land{level}_{step}"], order[step]))
        for level in range(levels):
            order = plan.order(level)
            top = s[f"top{level}"]
            here = index(order[: step + 1])
            copies[level].wait()
            top[here] = top[here] + s[f"land{level}_{step}"][...]
    own = index(plan.halved)
    for step, bit in enumerate(plan.rest):
        copies = [
            ship(s[f"top{level}"].at[own], s["rest"].at[step, level], bit)
            for level in range(levels)
        ]
        for level in range(levels):
            copies[level].wait()
            s[f"top{level}"][own] = s[f"top{level}"][own] + s["rest"][step, level]

    for level in range(levels):
        s["group"][me, level] = s[f"top{level}"][own]
    gather(s["group"])

    rows = n * chunk
    uses = [0]

    def total(value):
        for bit in plan.gbits:
            slot = uses[0]
            uses[0] += 1
            s["tot_out"][slot] = value
            ship(s["tot_out"].at[slot], s["tot_in"].at[slot], bit).wait()
            value = value + s["tot_in"][slot]
        return value

    inverses = [split(inverse_top[level]) for level in range(levels)]
    top_fwd = []
    for level in range(levels):
        residual = s["group"][:, level].reshape(rows, block)
        if level > 0:
            terms = 0.0
            for lower in range(level):
                terms = terms + mul(
                    split(top_fwd[lower]), split(upper_top[pair_index(level, lower)])
                )
            residual = residual - total(terms)
        top_fwd.append(mul(split(residual), inverses[level], NT))
    top_back = [None] * levels
    for level in reversed(range(levels)):
        residual = top_fwd[level]
        for higher in range(level + 1, levels):
            residual = residual - mul(
                split(top_back[higher]), split(upper_top[pair_index(higher, level)]), NT
            )
        top_back[level] = total(mul(split(residual), inverses[level]))
        s["answer"][level] = top_back[level].reshape(n, chunk, block)

    for step in reversed(range(len(plan.halved))):
        copies = []
        for level in range(levels):
            order = plan.order(level)
            mine = s[f"back{level}"]
            held = index(order[: step + 1])
            if step == len(plan.halved) - 1:
                mine[held] = s["answer"][level, me]
            copies.append(ship(mine.at[held], mine.at[held], order[step]))
        for copy in copies:
            copy.wait()

    residual = middle_fwd
    for level in range(levels):
        turned = s[f"back{level}"][...].reshape(columns, block)
        residual = residual - mul(split(upper_middle[level, 0, 0]), split(turned), NT)
    s["mid2"][...] = mul(split(inv_mid.T), split(residual)).reshape(n, share, columns)

    def fill_top(t):
        if t == nbits - 1:
            for level in range(levels):
                s["top_rows"][level] = s[f"back{level}"][...].reshape(columns, block).T
                start = pl.multiple_of(me * share, share)
                solve_top[level] = s["top_rows"][level, pl.ds(start, share), :]

    scatter_sum(s["mid2"], s["mid2_land"], fill_top)
    solve_middle[0, 0] = s["mid2"][me]
    s["mid2_full"][me] = s["mid2"][me]
    gather(s["mid2_full"])
    middle = split(s["mid2_full"][...].reshape(block, columns))
    leaf_res = s["leaf_fwd"][...] - kept * mul((s["low_high"][...], s["low_low"][...]), middle)
    solve_leaf[0, 0, 0] = mul((s["inv_high"][...], s["inv_low"][...]), split(leaf_res))


def scratch_list(plan):
    n, levels, block, columns, chunk = plan.n, plan.levels, plan.block, plan.columns, plan.chunk
    share = block // n
    f32, b16 = jnp.float32, jnp.bfloat16
    nh, nbits = len(plan.halved), len(plan.gbits)
    alls = nbits * (2 * levels)
    slots = 4 * (n - 1) + (2 * nh + len(plan.rest)) * levels + (n - 1) + alls
    out = [
        ("send", pltpu.SemaphoreType.DMA((slots,))),
        ("recv", pltpu.SemaphoreType.DMA((slots,))),
        ("leaf_fwd", pltpu.VMEM((block, columns), f32)),
        ("inv_high", pltpu.VMEM((block, block), b16)),
        ("inv_low", pltpu.VMEM((block, block), b16)),
        ("low_high", pltpu.VMEM((block, block), b16)),
        ("low_low", pltpu.VMEM((block, block), b16)),
        ("mid", pltpu.VMEM((n, share, columns), f32)),
        ("mid_land", pltpu.VMEM((n - 1, share, columns), f32)),
        ("mid_full", pltpu.VMEM((n, share, columns), f32)),
        ("mid2", pltpu.VMEM((n, share, columns), f32)),
        ("mid2_full", pltpu.VMEM((n, share, columns), f32)),
        ("mid2_land", pltpu.VMEM((n - 1, share, columns), f32)),
        ("group", pltpu.VMEM((n, levels, chunk, block), f32)),
        ("answer", pltpu.VMEM((levels, n, chunk, block), f32)),
        ("tot_out", pltpu.VMEM((alls, n * chunk, block), f32)),
        ("tot_in", pltpu.VMEM((alls, n * chunk, block), f32)),
        ("top_rows", pltpu.VMEM((levels, block, columns), f32)),
    ]
    if plan.rest:
        out.append(("rest", pltpu.VMEM((len(plan.rest), levels, chunk, block), f32)))
    for level in range(levels):
        out.append((f"top{level}", pltpu.VMEM((2,) * nh + (chunk, block), f32)))
        out.append((f"back{level}", pltpu.VMEM((2,) * nh + (chunk, block), f32)))
        for step in range(nh):
            shape = (2,) * (nh - step - 1) + (chunk, block)
            out.append((f"land{level}_{step}", pltpu.VMEM(shape, f32)))
    return out


def local(sizes, *args):
    right_leaf, right_middle, right_top = args[0], args[4], args[7]
    block, columns = right_leaf.shape[-2:]
    plan = Plan(sizes, right_top.shape[0], block, columns)
    vmem = pl.BlockSpec(memory_space=pltpu.VMEM)
    in_specs = [vmem] * len(args)
    in_specs[3] = pl.BlockSpec(memory_space=pltpu.SMEM)
    return pl.pallas_call(
        functools.partial(kernel, plan),
        out_shape=(
            jax.ShapeDtypeStruct(right_leaf.shape, jnp.float32),
            jax.ShapeDtypeStruct(right_middle.shape, jnp.float32),
            jax.ShapeDtypeStruct(right_top.shape, jnp.float32),
        ),
        in_specs=in_specs,
        out_specs=(vmem,) * 3,
        scratch_shapes=[shape for _, shape in scratch_list(plan)],
        compiler_params=pltpu.CompilerParams(
            collective_id=0, has_side_effects=True, vmem_limit_bytes=56 * 2**20
        ),
    )(*args)


def solution(mesh):
    in_specs = (
        P("leaf", "grow", "gcol", None, None),
        P("leaf", "grow", "gcol", None, None),
        P("leaf", "grow", "gcol", None, None),
        P("leaf", "grow", "gcol"),
        P("leaf", "grow", "gcol", None),
        P("leaf", "grow", "gcol", None),
        P(None, "leaf", "grow", "gcol", None),
        P(None, "gcol", None),
        P(None, "gcol", None),
        P(None, "gcol", None),
    )
    out_specs = (
        P("leaf", "grow", "gcol", None, None),
        P("leaf", "grow", "gcol", None),
        P(None, "gcol", None),
    )
    sizes = {axis: mesh.shape[axis] for axis in AXES}
    return jax.shard_map(
        functools.partial(local, sizes),
        mesh=mesh,
        in_specs=in_specs,
        out_specs=out_specs,
        check_vma=False,
    )
```

time: 333 us -> 92.9 us (0.28)
  waiting for transfers between devices: 283 us -> 0 us
  Pallas kernels: 0 us -> 87.9 us
  matrix products: 23.2 us -> 0 us
  between operations: 15.2 us -> 1.3 us
    psum x6 -> x0, waiting for transfers between devices: 260 us -> none  [the longest x1 93.4 us: combine_layers(): stacked = lax.psum(stacked * row_keep, ('grow', 'gcol'))]
    pallas_call x0 -> x1, Pallas kernels: none -> 87.9 us  [local(): pl.pallas_call(functools.partial(kernel, plan), out_shape=(jax.ShapeDtype...]
    dot_general x16 -> x0, matrix products: 23.2 us -> none  [the longest x8 12.7 us: product(): jnp.dot(factor, vector, precision=PRECISE, preferred_element_type=jnp.flo...]
    ppermute x1 -> x0, waiting for transfers between devices: 23 us -> none  [from_partner(): return lax.ppermute(value, axis, pairs)]
  transfers between devices with their start and end apart: 7 -> 0, of which waited for: 7 -> 0; matrix products, arithmetic and copies ran while one was open for 0% -> 0% of each run, Pallas kernels for 0% -> 0%
where the time goes in v1:
time: 92.9 us; the launch traced here: 92.8 us
  Pallas kernels  87.9 us (95%)
  local copies, waits for them, and re-layouts  3.61 us (4%)
  between operations  1.3 us (1%)
    pallas_call x1, Pallas kernels, local(): pl.pallas_call(functools.partial(kernel, plan), out_shape=(jax.ShapeDtype...  87.9 us
    unnamed x7, local copies, waits for them, and re-layouts  3.61 us

profile of v1, /device:TPU:0, one launch (start us, length us, event | category | flops | bytes accessed | tf_op | source)
XLA Modules:
  0.0 92.8 jit_solution(833269321744252247)
XLA Ops:
  1.3 87.9 %shard_map.121 = (f32[1,1,1,512,256]{4,3,2,1,0:T(8,128)}, f32[1,1,128,256]{3,2,1,0:T(8,128)}, f32[2,128,256]{2,1,0:T(8,128)}) custom-call(f32[1,1,1,512,256]{4,3,2,1,0:T(8,128)} %right_leaf.1, f32[1,1,1,512,512]{4,3,2,1,0:T(8,128)} %inverse_leaf.1, f32[1,1,1,512,512]{4,3,2,1,0:T(8,128)} %lower_leaf.1, s32[1,1,1]{2,1,0:T(1,128)S(6)} %copy.16.present, ...), custom_call_target="tpu_custom_call" | custom-call | tf_op jit(solution)/shard_map/pallas_call | solution.py:330
  89.1 0.0 copy-start.1
  89.2 1.9 %copy.17 = f32[1,1,1,512,256]{4,3,2,1,0:T(8,128)} copy(f32[1,1,1,512,256]{4,3,2,1,0:T(8,128)} %get-tuple-element.6) | data formatting | bytes 1048576
  91.1 0.0 copy-done.1
  91.1 0.0 copy-start
  91.1 0.7 copy.18
  91.7 0.3 copy-done
  92.1 0.7 copy.19
Async XLA Ops:
  89.1 1.9 %copy-start.1 = (f32[1,1,128,256]{3,2,1,0:T(8,128)S(1)}, f32[1,1,128,256]{3,2,1,0:T(8,128)}, u32[]{:S(2)}) copy-start(f32[1,1,128,256]{3,2,1,0:T(8,128)} %get-tuple-element.7) | copy-start | bytes 393220
  91.1 1.0 %copy-start = (f32[2,128,256]{2,1,0:T(8,128)S(1)}, f32[2,128,256]{2,1,0:T(8,128)}, u32[]{:S(2)}) copy-start(f32[2,128,256]{2,1,0:T(8,128)} %get-tuple-element.8) | copy-start | bytes 786436

commit v2 on v1

v2 whole, which is shorter than its diff:
```python
import functools

import jax
import jax.numpy as jnp
from jax import lax
from jax.experimental import pallas as pl
from jax.experimental.pallas import tpu as pltpu
from jax.sharding import PartitionSpec as P

PARTS = 2
AXES = ("gcol", "leaf", "grow")
NN = ((1,), (0,))
NT = ((1,), (1,))


def pair_index(upper_level, lower_level):
    return upper_level * (upper_level - 1) // 2 + lower_level


def split(value):
    high = value.astype(jnp.bfloat16)
    low = (value - high.astype(jnp.float32)).astype(jnp.bfloat16)
    return high, low


def mul(left, right, dims=NN):
    def dot(a, b):
        return lax.dot_general(a, b, (dims, ((), ())), preferred_element_type=jnp.float32)

    return dot(left[0], right[0]) + (dot(left[0], right[1]) + dot(left[1], right[0]))


class Plan:
    def __init__(self, sizes, levels, block, columns):
        self.sizes, self.levels, self.block = sizes, levels, block
        self.parts = PARTS
        self.columns, self.width = columns, columns // PARTS
        self.n = sizes["gcol"]
        self.gbits = [("gcol", t) for t in range(self.n.bit_length() - 1)]
        others = [(a, t) for a in AXES[1:] for t in range(sizes[a].bit_length() - 1)]
        self.bits = self.gbits + others
        count = 0
        while count < len(self.bits) and self.width >> (count + 1) >= 8:
            count += 1
        self.halved, self.rest = self.bits[:count], self.bits[count:]
        self.chunk = self.width >> count
        first = self.gbits[:1]
        self.orders = [
            self.halved,
            first
            + [b for b in self.halved if b[0] == "leaf"]
            + [b for b in self.halved if b[0] == "gcol" and b not in first]
            + [b for b in self.halved if b[0] == "grow"],
        ]
        self.mats = levels + levels * (levels - 1) // 2

    def order(self, level):
        return self.orders[level % 2]

    def slots(self):
        n, nx = self.n, self.n // 2
        middle = 4 * (n - 1)
        top = (2 * len(self.halved) + len(self.rest)) * self.levels
        spread = self.mats * (1 + 4 * (nx - 1))
        return self.parts * (middle + top) + spread


def kernel(
    plan,
    right_leaf,
    inverse_leaf,
    lower_leaf,
    present,
    right_middle,
    inverse_middle,
    upper_middle,
    right_top,
    inverse_top,
    upper_top,
    solve_leaf,
    solve_middle,
    solve_top,
    *scratch,
):
    names = [name for name, _ in scratch_list(plan)]
    s = dict(zip(names, scratch))
    send, recv = s["send"], s["recv"]
    n, levels, block, chunk, width = plan.n, plan.levels, plan.block, plan.chunk, plan.width
    share = block // n
    nbits = len(plan.gbits)
    place = {axis: lax.axis_index(axis) for axis in AXES}
    me = place["gcol"]
    counter = [0]

    def bit_of(bit):
        return (place[bit[0]] // 2 ** bit[1]) % 2

    def partner(bit):
        return {bit[0]: place[bit[0]] + (1 - 2 * bit_of(bit)) * 2 ** bit[1]}

    def ship(source, target, where):
        slot = counter[0]
        counter[0] += 1
        copy = pltpu.make_async_remote_copy(
            src_ref=source,
            dst_ref=target,
            send_sem=send.at[slot],
            recv_sem=recv.at[slot],
            device_id=where,
            device_id_type=pl.DeviceIdType.MESH,
        )
        copy.start()
        return copy

    nx = n // 2
    core, row_x = me % 2, me // 2
    half_rows = share // 2
    mate, opposite = partner(("gcol", 0)), partner(("leaf", 0))
    half = bit_of(("leaf", 0))
    tops = s["tops"]
    offsets = range(1, nx)

    barrier = pltpu.get_barrier_semaphore()
    far = [{"gcol": (row_x + d) % nx * 2 + core} for d in offsets]
    greeted = [partner(bit) for bit in plan.bits if bit[0] != "gcol" or bit[1] == 0] + far
    for device in greeted:
        pl.semaphore_signal(
            barrier, inc=1, device_id=device, device_id_type=pl.DeviceIdType.MESH
        )
    for level in range(levels):
        tops[level, me] = inverse_top[level].reshape(2, half_rows, block)
    for pair in range(plan.mats - levels):
        tops[levels + pair, me] = upper_top[pair].reshape(2, half_rows, block)
    pl.semaphore_wait(barrier, len(greeted))

    first, second = list(range(levels)), list(range(levels, plan.mats))
    across, over, mated = {}, {}, []

    def came_from(d):
        return (row_x - d + nx) % nx * 2 + core

    def send_across(mats):
        for m in mats:
            mine = tops.at[m, me, half]
            across[m] = [ship(mine, mine, device) for device in far]

    def send_over(mats):
        for m in mats:
            over[m] = []
            for d, copy in zip(offsets, across[m]):
                copy.wait()
                piece = tops.at[m, came_from(d), half]
                over[m].append(ship(piece, piece, opposite))
                mated.append(ship(piece, piece, mate))

    def end_over(mats):
        for m in mats:
            for d, copy in zip(offsets, over[m]):
                copy.wait()
                piece = tops.at[m, came_from(d), 1 - half]
                mated.append(ship(piece, piece, mate))

    send_across(first)
    for m in first + second:
        mated.append(ship(tops.at[m, me], tops.at[m, me], mate))
    done = set()

    def once(name, act):
        if name not in done:
            done.add(name)
            act()

    kept = present[0, 0, 0].astype(jnp.float32)
    leaf_fwd = mul(split(inverse_leaf[0, 0, 0]), split(right_leaf[0, 0, 0]))
    s["leaf_fwd"][...] = leaf_fwd
    lower_pair = split(lower_leaf[0, 0, 0])
    inv_mid = inverse_middle[0, 0]
    lead = ((place["leaf"] + place["grow"]) == 0).astype(jnp.float32)
    bits_shape = (2,) * len(plan.halved)

    def fill_inverse():
        high, low = split(inverse_leaf[0, 0, 0].T)
        s["inv_high"][...] = high
        s["inv_low"][...] = low

    def fill_lower():
        high, low = split(lower_leaf[0, 0, 0].T)
        s["low_high"][...] = high
        s["low_low"][...] = low

    def split_tops():
        for m in range(plan.mats):
            high, low = split(tops[m].reshape(block, block))
            s["top_high"][m] = high
            s["top_low"][m] = low

    def narrow(value, m, dims):
        rest = value - value.astype(jnp.bfloat16).astype(jnp.float32)
        both = jnp.concatenate([value, rest], axis=0).astype(jnp.bfloat16)
        high, low = s["top_high"][m], s["top_low"][m]

        def dot(a, b):
            return lax.dot_general(a, b, (dims, ((), ())), preferred_element_type=jnp.float32)

        wide = dot(both, high)
        return wide[:chunk] + (wide[chunk:] + dot(both, low)[:chunk])

    def index(known, bit=None, flip=False):
        where = []
        for b in plan.halved:
            if b in known:
                where.append(bit_of(b))
            elif b == bit:
                where.append(1 - bit_of(b) if flip else bit_of(b))
            else:
                where.append(slice(None))
        return tuple(where)

    def scatter_sum(blocks, landing):
        at = 0
        for t, bit in enumerate(plan.gbits):
            low = me % 2**t
            count = n >> (t + 1)
            theirs = low + (1 - bit_of(bit)) * 2**t
            mine = low + bit_of(bit) * 2**t
            copies = [
                ship(blocks.at[theirs + j * 2 ** (t + 1)], landing.at[at + j], partner(bit))
                for j in range(count)
            ]
            yield
            for j, copy in enumerate(copies):
                copy.wait()
                where = mine + j * 2 ** (t + 1)
                blocks[where] = blocks[where] + landing[at + j]
            at += count

    def gather(blocks):
        for t in reversed(range(nbits)):
            low = me % 2 ** (t + 1)
            copies = [
                ship(*(blocks.at[low + j * 2 ** (t + 1)],) * 2, partner(plan.gbits[t]))
                for j in range(n >> (t + 1))
            ]
            yield
            for copy in copies:
                copy.wait()

    def pipeline(p):
        cols = slice(p * width, (p + 1) * width)
        own = index(plan.halved)
        mid, mid_full = s["mid"].at[p], s["mid_full"].at[p]
        part = mul(lower_pair, split(s["leaf_fwd"][:, cols])) * kept
        mid[...] = part.reshape(n, share, width)
        steps = scatter_sum(mid, s["mid_land"].at[p])
        next(steps)
        once("inverse", fill_inverse)
        yield
        for _ in steps:
            once("lower", fill_lower)
            yield
        mid_full[me] = right_middle[0, 0, :, cols] - mid[me]
        steps = gather(mid_full)
        next(steps)
        once("over", lambda: send_over(first))
        yield
        yield from steps
        middle_fwd = mul(split(inv_mid), split(mid_full[...].reshape(block, width)))
        s["middle_fwd"][p] = middle_fwd

        fwd_turned = split(middle_fwd.T)
        for level in range(levels):
            turned = mul(fwd_turned, split(upper_middle[level, 0, 0]))
            right = right_top[level, :, cols].T * lead
            placed = jnp.concatenate(
                [right * (me == c).astype(jnp.float32) for c in range(n)], axis=1
            )
            s[f"top{p}_{level}"][...] = (placed - turned).reshape(bits_shape + (chunk, block))
        for step in range(len(plan.halved)):
            copies = []
            for level in range(levels):
                order = plan.order(level)
                there = index(order[:step], order[step], True)
                copies.append(
                    ship(
                        s[f"top{p}_{level}"].at[there],
                        s[f"land{p}_{level}_{step}"],
                        partner(order[step]),
                    )
                )
            if step == 0:
                once("across", lambda: send_across(second))
            if step == 1:
                once("end", lambda: end_over(first))
            if step == 3:
                once("over2", lambda: send_over(second))
            yield
            for level in range(levels):
                here = index(plan.order(level)[: step + 1])
                top = s[f"top{p}_{level}"]
                copies[level].wait()
                top[here] = top[here] + s[f"land{p}_{level}_{step}"][...]
        for step, bit in enumerate(plan.rest):
            copies = [
                ship(
                    s[f"top{p}_{level}"].at[own],
                    s[f"rest{p}"].at[step, level],
                    partner(bit),
                )
                for level in range(levels)
            ]
            once("over2", lambda: send_over(second))
            once("end2", lambda: end_over(second))
            yield
            for level in range(levels):
                top = s[f"top{p}_{level}"]
                copies[level].wait()
                top[own] = top[own] + s[f"rest{p}"][step, level]

        def finish_tops():
            once("over2", lambda: send_over(second))
            once("end2", lambda: end_over(second))
            for copy in mated:
                copy.wait()
            split_tops()

        once("tops", finish_tops)
        top_fwd = []
        for level in range(levels):
            residual = s[f"top{p}_{level}"][own]
            for lower in range(level):
                m = levels + pair_index(level, lower)
                residual = residual - narrow(top_fwd[lower], m, NN)
            top_fwd.append(narrow(residual, level, NT))
        top_back = [None] * levels
        for level in reversed(range(levels)):
            residual = top_fwd[level]
            for higher in range(level + 1, levels):
                m = levels + pair_index(higher, level)
                residual = residual - narrow(top_back[higher], m, NT)
            top_back[level] = narrow(residual, level, NN)
            s[f"back{p}_{level}"][own] = top_back[level]
        for step in reversed(range(len(plan.halved))):
            copies = []
            for level in range(levels):
                order = plan.order(level)
                held = s[f"back{p}_{level}"].at[index(order[: step + 1])]
                copies.append(ship(held, held, partner(order[step])))
            yield
            for copy in copies:
                copy.wait()

        residual = s["middle_fwd"][p]
        for level in range(levels):
            turned = s[f"back{p}_{level}"][...].reshape(width, block)
            residual = residual - mul(split(upper_middle[level, 0, 0]), split(turned), NT)
        mid2, mid2_full = s["mid2"].at[p], s["mid2_full"].at[p]
        mid2[...] = mul(split(inv_mid.T), split(residual)).reshape(n, share, width)
        steps = scatter_sum(mid2, s["mid2_land"].at[p])
        next(steps)
        for level in range(levels):
            rows = s["top_rows"].at[level]
            rows[...] = s[f"back{p}_{level}"][...].reshape(width, block).T
            solve_top[level, :, cols] = rows[pl.ds(pl.multiple_of(me * share, share), share), :]
        yield
        yield from steps
        solve_middle[0, 0, :, cols] = mid2[me]
        mid2_full[me] = mid2[me]
        yield from gather(mid2_full)
        middle = split(mid2_full[...].reshape(block, width))
        leaf_res = s["leaf_fwd"][:, cols] - kept * mul(
            (s["low_high"][...], s["low_low"][...]), middle
        )
        solve_leaf[0, 0, 0, :, cols] = mul((s["inv_high"][...], s["inv_low"][...]), split(leaf_res))

    running = [pipeline(p) for p in range(plan.parts)]
    while running:
        running = [steps for steps in running if next(steps, StopIteration) is not StopIteration]


def scratch_list(plan):
    n, levels, block, width, chunk = plan.n, plan.levels, plan.block, plan.width, plan.chunk
    share, parts = block // n, plan.parts
    f32, b16 = jnp.float32, jnp.bfloat16
    nh, slots = len(plan.halved), plan.slots()
    out = [
        ("send", pltpu.SemaphoreType.DMA((slots,))),
        ("recv", pltpu.SemaphoreType.DMA((slots,))),
        ("leaf_fwd", pltpu.VMEM((block, plan.columns), f32)),
        ("inv_high", pltpu.VMEM((block, block), b16)),
        ("inv_low", pltpu.VMEM((block, block), b16)),
        ("low_high", pltpu.VMEM((block, block), b16)),
        ("low_low", pltpu.VMEM((block, block), b16)),
        ("mid", pltpu.VMEM((parts, n, share, width), f32)),
        ("mid_land", pltpu.VMEM((parts, n - 1, share, width), f32)),
        ("mid_full", pltpu.VMEM((parts, n, share, width), f32)),
        ("middle_fwd", pltpu.VMEM((parts, share, width), f32)),
        ("mid2", pltpu.VMEM((parts, n, share, width), f32)),
        ("mid2_full", pltpu.VMEM((parts, n, share, width), f32)),
        ("mid2_land", pltpu.VMEM((parts, n - 1, share, width), f32)),
        ("tops", pltpu.VMEM((plan.mats, n, 2, share // 2, block), f32)),
        ("top_high", pltpu.VMEM((plan.mats, block, block), b16)),
        ("top_low", pltpu.VMEM((plan.mats, block, block), b16)),
        ("top_rows", pltpu.VMEM((levels, block, width), f32)),
    ]
    for p in range(parts):
        if plan.rest:
            out.append((f"rest{p}", pltpu.VMEM((len(plan.rest), levels, chunk, block), f32)))
        for level in range(levels):
            out.append((f"top{p}_{level}", pltpu.VMEM((2,) * nh + (chunk, block), f32)))
            out.append((f"back{p}_{level}", pltpu.VMEM((2,) * nh + (chunk, block), f32)))
            for step in range(nh):
                shape = (2,) * (nh - step - 1) + (chunk, block)
                out.append((f"land{p}_{level}_{step}", pltpu.VMEM(shape, f32)))
    return out


def copy_out(*refs):
    count = len(refs) // 2
    sems = refs[-1]
    copies = [
        pltpu.make_async_copy(refs[i], refs[count + i], sems.at[i]) for i in range(count)
    ]
    for copy in copies:
        copy.start()
    for copy in copies:
        copy.wait()


def local(sizes, *args):
    right_leaf, right_middle, right_top = args[0], args[4], args[7]
    block, columns = right_leaf.shape[-2:]
    plan = Plan(sizes, right_top.shape[0], block, columns)
    vmem = pl.BlockSpec(memory_space=pltpu.VMEM)
    in_specs = [vmem] * len(args)
    in_specs[3] = pl.BlockSpec(memory_space=pltpu.SMEM)
    solved = pl.pallas_call(
        functools.partial(kernel, plan),
        out_shape=(
            jax.ShapeDtypeStruct(right_leaf.shape, jnp.float32),
            jax.ShapeDtypeStruct(right_middle.shape, jnp.float32),
            jax.ShapeDtypeStruct(right_top.shape, jnp.float32),
        ),
        in_specs=in_specs,
        out_specs=(vmem,) * 3,
        scratch_shapes=[shape for _, shape in scratch_list(plan)],
        compiler_params=pltpu.CompilerParams(
            collective_id=0, has_side_effects=True, vmem_limit_bytes=56 * 2**20
        ),
    )(*args)
    anywhere = pl.BlockSpec(memory_space=pl.ANY)
    return pl.pallas_call(
        copy_out,
        out_shape=tuple(jax.ShapeDtypeStruct(x.shape, x.dtype) for x in solved),
        in_specs=[anywhere] * len(solved),
        out_specs=(anywhere,) * len(solved),
        scratch_shapes=[pltpu.SemaphoreType.DMA((len(solved),))],
    )(*solved)


def solution(mesh):
    in_specs = (
        P("leaf", "grow", "gcol", None, None),
        P("leaf", "grow", "gcol", None, None),
        P("leaf", "grow", "gcol", None, None),
        P("leaf", "grow", "gcol"),
        P("leaf", "grow", "gcol", None),
        P("leaf", "grow", "gcol", None),
        P(None, "leaf", "grow", "gcol", None),
        P(None, "gcol", None),
        P(None, "gcol", None),
        P(None, "gcol", None),
    )
    out_specs = (
        P("leaf", "grow", "gcol", None, None),
        P("leaf", "grow", "gcol", None),
        P(None, "gcol", None),
    )
    sizes = {axis: mesh.shape[axis] for axis in AXES}
    return jax.shard_map(
        functools.partial(local, sizes),
        mesh=mesh,
        in_specs=in_specs,
        out_specs=out_specs,
        check_vma=False,
    )
```

time: 92.9 us -> 98.2 us (1.057)
  Pallas kernels: 87.9 us -> 96.7 us
  local copies, waits for them, and re-layouts: 3.61 us -> 0 us
    pallas_call x0 -> x1, Pallas kernels: none -> 28.9 us  [local(): pl.pallas_call(copy_out, out_shape=tuple((jax.ShapeDtypeStruct(x.shape, x...]
    pallas_call x1, Pallas kernels: 87.9 us -> 67.8 us  [local(): pl.pallas_call(functools.partial(kernel, plan), out_shape=(jax.ShapeDtype...]
    unnamed x7 -> x0, local copies, waits for them, and re-layouts: 3.61 us -> none
where the time goes in v2:
time: 98.2 us; the launch traced here: 98 us
  Pallas kernels  96.7 us (98%)
  between operations  1.29 us (1%)
    pallas_call x1, Pallas kernels, local(): pl.pallas_call(functools.partial(kernel, plan), out_shape=(jax.ShapeDtype...  67.8 us
    pallas_call x1, Pallas kernels, local(): pl.pallas_call(copy_out, out_shape=tuple((jax.ShapeDtypeStruct(x.shape, x...  28.9 us

profile of v2, /device:TPU:0, one launch (start us, length us, event | category | flops | bytes accessed | tf_op | source)
XLA Modules:
  0.0 98.0 jit_solution(10728495024508314751)
XLA Ops:
  1.3 67.8 %shard_map.121 = (f32[1,1,1,512,256]{4,3,2,1,0:T(8,128)}, f32[1,1,128,256]{3,2,1,0:T(8,128)}, f32[2,128,256]{2,1,0:T(8,128)}) custom-call(f32[1,1,1,512,256]{4,3,2,1,0:T(8,128)} %right_leaf.1, f32[1,1,1,512,512]{4,3,2,1,0:T(8,128)} %inverse_leaf.1, f32[1,1,1,512,512]{4,3,2,1,0:T(8,128)} %lower_leaf.1, s32[1,1,1]{2,1,0:T(1,128)S(6)} %copy.13.present, ...), custom_call_target="tpu_custom_call" | custom-call | tf_op jit(solution)/shard_map/pallas_call | solution.py:436
  69.1 28.9 %shard_map.122 = (f32[1,1,1,512,256]{4,3,2,1,0:T(8,128)}, f32[1,1,128,256]{3,2,1,0:T(8,128)}, f32[2,128,256]{2,1,0:T(8,128)}) custom-call(f32[1,1,1,512,256]{4,3,2,1,0:T(8,128)} %get-tuple-element.6.refs_0_, f32[1,1,128,256]{3,2,1,0:T(8,128)} %get-tuple-element.7.refs_1_, f32[2,128,256]{2,1,0:T(8,128)} %get-tuple-element.8.refs_2_), custom_call_target="tpu_custom_call" | custom-call | tf_op jit(solution)/shard_map/pallas_call | solution.py:451

commit v3 on v2

--- a/solution.py
+++ b/solution.py
@@ -61,7 +61,7 @@
         n, nx = self.n, self.n // 2
         middle = 4 * (n - 1)
         top = (2 * len(self.halved) + len(self.rest)) * self.levels
-        spread = self.mats * (1 + 4 * (nx - 1))
+        spread = self.mats * (1 + 5 * (nx - 1))
         return self.parts * (middle + top) + spread
 
 
@@ -114,9 +114,9 @@
 
     nx = n // 2
     core, row_x = me % 2, me // 2
-    half_rows = share // 2
-    mate, opposite = partner(("gcol", 0)), partner(("leaf", 0))
-    half = bit_of(("leaf", 0))
+    quarter_rows = share // 4
+    mate, opposite, above = partner(("gcol", 0)), partner(("leaf", 0)), partner(("grow", 0))
+    leaf_bit, grow_bit = bit_of(("leaf", 0)), bit_of(("grow", 0))
     tops = s["tops"]
     offsets = range(1, nx)
 
@@ -128,40 +128,40 @@
             barrier, inc=1, device_id=device, device_id_type=pl.DeviceIdType.MESH
         )
     for level in range(levels):
-        tops[level, me] = inverse_top[level].reshape(2, half_rows, block)
+        tops[level, me] = inverse_top[level].reshape(2, 2, quarter_rows, block)
     for pair in range(plan.mats - levels):
-        tops[levels + pair, me] = upper_top[pair].reshape(2, half_rows, block)
+        tops[levels + pair, me] = upper_top[pair].reshape(2, 2, quarter_rows, block)
     pl.semaphore_wait(barrier, len(greeted))
 
-    first, second = list(range(levels)), list(range(levels, plan.mats))
-    across, over, mated = {}, {}, []
-
-    def came_from(d):
-        return (row_x - d + nx) % nx * 2 + core
-
-    def send_across(mats):
-        for m in mats:
-            mine = tops.at[m, me, half]
-            across[m] = [ship(mine, mine, device) for device in far]
-
-    def send_over(mats):
-        for m in mats:
-            over[m] = []
-            for d, copy in zip(offsets, across[m]):
-                copy.wait()
-                piece = tops.at[m, came_from(d), half]
-                over[m].append(ship(piece, piece, opposite))
-                mated.append(ship(piece, piece, mate))
-
-    def end_over(mats):
-        for m in mats:
-            for d, copy in zip(offsets, over[m]):
-                copy.wait()
-                piece = tops.at[m, came_from(d), 1 - half]
-                mated.append(ship(piece, piece, mate))
-
-    send_across(first)
-    for m in first + second:
+    mats = range(plan.mats)
+    across, over, up, mated = [], [], [], []
+
+    def pieces():
+        return [(m, (row_x - d + nx) % nx * 2 + core) for m in mats for d in offsets]
+
+    def send_over():
+        for (m, source), copy in zip(pieces(), across):
+            copy.wait()
+            piece = tops.at[m, source, grow_bit, leaf_bit]
+            over.append(ship(piece, piece, opposite))
+
+    def send_up():
+        for (m, source), copy in zip(pieces(), over):
+            copy.wait()
+            piece = tops.at[m, source, grow_bit]
+            up.append(ship(piece, piece, above))
+            mated.append(ship(piece, piece, mate))
+
+    def end_up():
+        for (m, source), copy in zip(pieces(), up):
+            copy.wait()
+            piece = tops.at[m, source, 1 - grow_bit]
+            mated.append(ship(piece, piece, mate))
+
+    for m in mats:
+        mine = tops.at[m, me, grow_bit, leaf_bit]
+        across += [ship(mine, mine, device) for device in far]
+    for m in mats:
         mated.append(ship(tops.at[m, me], tops.at[m, me], mate))
     done = set()
 
@@ -174,7 +174,6 @@
     leaf_fwd = mul(split(inverse_leaf[0, 0, 0]), split(right_leaf[0, 0, 0]))
     s["leaf_fwd"][...] = leaf_fwd
     lower_pair = split(lower_leaf[0, 0, 0])
-    inv_mid = inverse_middle[0, 0]
     lead = ((place["leaf"] + place["grow"]) == 0).astype(jnp.float32)
     bits_shape = (2,) * len(plan.halved)
 
@@ -187,12 +186,33 @@
         high, low = split(lower_leaf[0, 0, 0].T)
         s["low_high"][...] = high
         s["low_low"][...] = low
+
+    def keep(name, pair, *where):
+        for kind, value in zip(("high", "low"), pair):
+            s[f"{name}_{kind}"][(*where, Ellipsis)] = value
+
+    def kept_pair(name, *where):
+        return tuple(s[f"{name}_{kind}"][(*where, Ellipsis)] for kind in ("high", "low"))
+
+    def fill_middle():
+        keep("im", split(inverse_middle[0, 0]))
+        for level in range(levels):
+            keep("um", split(upper_middle[level, 0, 0]), level)
+
+    def fill_middle_turned():
+        keep("imt", split(inverse_middle[0, 0].T))
 
     def split_tops():
         for m in range(plan.mats):
             high, low = split(tops[m].reshape(block, block))
             s["top_high"][m] = high
             s["top_low"][m] = low
+
+    def finish_tops():
+        end_up()
+        for copy in mated:
+            copy.wait()
+        split_tops()
 
     def narrow(value, m, dims):
         rest = value - value.astype(jnp.bfloat16).astype(jnp.float32)
@@ -251,25 +271,24 @@
         mid, mid_full = s["mid"].at[p], s["mid_full"].at[p]
         part = mul(lower_pair, split(s["leaf_fwd"][:, cols])) * kept
         mid[...] = part.reshape(n, share, width)
-        steps = scatter_sum(mid, s["mid_land"].at[p])
-        next(steps)
-        once("inverse", fill_inverse)
-        yield
-        for _ in steps:
-            once("lower", fill_lower)
+        for t, _ in enumerate(scatter_sum(mid, s["mid_land"].at[p])):
+            if t == nbits - 1:
+                once("middle", fill_middle)
+                once("lower", fill_lower)
             yield
         mid_full[me] = right_middle[0, 0, :, cols] - mid[me]
-        steps = gather(mid_full)
-        next(steps)
-        once("over", lambda: send_over(first))
-        yield
-        yield from steps
-        middle_fwd = mul(split(inv_mid), split(mid_full[...].reshape(block, width)))
+        for t, _ in enumerate(gather(mid_full)):
+            if t == 0:
+                once("over", send_over)
+                once("inverse", fill_inverse)
+            yield
+        once("up", send_up)
+        middle_fwd = mul(kept_pair("im"), split(mid_full[...].reshape(block, width)))
         s["middle_fwd"][p] = middle_fwd
 
         fwd_turned = split(middle_fwd.T)
         for level in range(levels):
-            turned = mul(fwd_turned, split(upper_middle[level, 0, 0]))
+            turned = mul(fwd_turned, kept_pair("um", level))
             right = right_top[level, :, cols].T * lead
             placed = jnp.concatenate(
                 [right * (me == c).astype(jnp.float32) for c in range(n)], axis=1
@@ -287,12 +306,6 @@
                         partner(order[step]),
                     )
                 )
-            if step == 0:
-                once("across", lambda: send_across(second))
-            if step == 1:
-                once("end", lambda: end_over(first))
-            if step == 3:
-                once("over2", lambda: send_over(second))
             yield
             for level in range(levels):
                 here = index(plan.order(level)[: step + 1])
@@ -308,20 +321,12 @@
                 )
                 for level in range(levels)
             ]
-            once("over2", lambda: send_over(second))
-            once("end2", lambda: end_over(second))
+            once("tops", finish_tops)
             yield
             for level in range(levels):
                 top = s[f"top{p}_{level}"]
                 copies[level].wait()
                 top[own] = top[own] + s[f"rest{p}"][step, level]
-
-        def finish_tops():
-            once("over2", lambda: send_over(second))
-            once("end2", lambda: end_over(second))
-            for copy in mated:
-                copy.wait()
-            split_tops()
 
         once("tops", finish_tops)
         top_fwd = []
@@ -345,6 +350,7 @@
                 order = plan.order(level)
                 held = s[f"back{p}_{level}"].at[index(order[: step + 1])]
                 copies.append(ship(held, held, partner(order[step])))
+            once("turned", fill_middle_turned)
             yield
             for copy in copies:
                 copy.wait()
@@ -352,9 +358,9 @@
         residual = s["middle_fwd"][p]
         for level in range(levels):
             turned = s[f"back{p}_{level}"][...].reshape(width, block)
-            residual = residual - mul(split(upper_middle[level, 0, 0]), split(turned), NT)
+            residual = residual - mul(kept_pair("um", level), split(turned), NT)
         mid2, mid2_full = s["mid2"].at[p], s["mid2_full"].at[p]
-        mid2[...] = mul(split(inv_mid.T), split(residual)).reshape(n, share, width)
+        mid2[...] = mul(kept_pair("imt"), split(residual)).reshape(n, share, width)
         steps = scatter_sum(mid2, s["mid2_land"].at[p])
         next(steps)
         for level in range(levels):
@@ -390,6 +396,12 @@
         ("inv_low", pltpu.VMEM((block, block), b16)),
         ("low_high", pltpu.VMEM((block, block), b16)),
         ("low_low", pltpu.VMEM((block, block), b16)),
+        ("im_high", pltpu.VMEM((share, block), b16)),
+        ("im_low", pltpu.VMEM((share, block), b16)),
+        ("imt_high", pltpu.VMEM((block, share), b16)),
+        ("imt_low", pltpu.VMEM((block, share), b16)),
+        ("um_high", pltpu.VMEM((levels, share, block), b16)),
+        ("um_low", pltpu.VMEM((levels, share, block), b16)),
         ("mid", pltpu.VMEM((parts, n, share, width), f32)),
         ("mid_land", pltpu.VMEM((parts, n - 1, share, width), f32)),
         ("mid_full", pltpu.VMEM((parts, n, share, width), f32)),
@@ -397,7 +409,7 @@
         ("mid2", pltpu.VMEM((parts, n, share, width), f32)),
         ("mid2_full", pltpu.VMEM((parts, n, share, width), f32)),
         ("mid2_land", pltpu.VMEM((parts, n - 1, share, width), f32)),
-        ("tops", pltpu.VMEM((plan.mats, n, 2, share // 2, block), f32)),
+        ("tops", pltpu.VMEM((plan.mats, n, 2, 2, share // 4, block), f32)),
         ("top_high", pltpu.VMEM((plan.mats, block, block), b16)),
         ("top_low", pltpu.VMEM((plan.mats, block, block), b16)),
         ("top_rows", pltpu.VMEM((levels, block, width), f32)),
@@ -416,14 +428,8 @@
 
 def copy_out(*refs):
     count = len(refs) // 2
-    sems = refs[-1]
-    copies = [
-        pltpu.make_async_copy(refs[i], refs[count + i], sems.at[i]) for i in range(count)
-    ]
-    for copy in copies:
-        copy.start()
-    for copy in copies:
-        copy.wait()
+    for source, target in zip(refs[:count], refs[count:]):
+        target[...] = source[...]
 
 
 def local(sizes, *args):
@@ -447,13 +453,11 @@
             collective_id=0, has_side_effects=True, vmem_limit_bytes=56 * 2**20
         ),
     )(*args)
-    anywhere = pl.BlockSpec(memory_space=pl.ANY)
     return pl.pallas_call(
         copy_out,
         out_shape=tuple(jax.ShapeDtypeStruct(x.shape, x.dtype) for x in solved),
-        in_specs=[anywhere] * len(solved),
-        out_specs=(anywhere,) * len(solved),
-        scratch_shapes=[pltpu.SemaphoreType.DMA((len(solved),))],
+        in_specs=[vmem] * len(solved),
+        out_specs=(vmem,) * len(solved),
     )(*solved)
 
 

time: 98.2 us -> 68.7 us (0.70)
  Pallas kernels: 96.7 us -> 67.2 us
    pallas_call x1, Pallas kernels: 28.9 us -> 2.11 us  [local(): pl.pallas_call(copy_out, out_shape=tuple((jax.ShapeDtypeStruct(x.shape, x...]
    pallas_call x1, Pallas kernels: 67.8 us -> 65.1 us  [local(): pl.pallas_call(functools.partial(kernel, plan), out_shape=(jax.ShapeDtype...]
where the time goes in v3:
time: 68.7 us; the launch traced here: 68.5 us
  Pallas kernels  67.2 us (98%)
  between operations  1.29 us (2%)
    pallas_call x1, Pallas kernels, local(): pl.pallas_call(functools.partial(kernel, plan), out_shape=(jax.ShapeDtype...  65.1 us
    pallas_call x1, Pallas kernels, local(): pl.pallas_call(copy_out, out_shape=tuple((jax.ShapeDtypeStruct(x.shape, x...  2.11 us

profile of v3, /device:TPU:0, one launch (start us, length us, event | category | flops | bytes accessed | tf_op | source)
XLA Modules:
  0.0 68.5 jit_solution(3663802702653672998)
XLA Ops:
  1.3 65.1 %shard_map.121 = (f32[1,1,1,512,256]{4,3,2,1,0:T(8,128)}, f32[1,1,128,256]{3,2,1,0:T(8,128)}, f32[2,128,256]{2,1,0:T(8,128)}) custom-call(f32[1,1,1,512,256]{4,3,2,1,0:T(8,128)} %right_leaf.1, f32[1,1,1,512,512]{4,3,2,1,0:T(8,128)} %inverse_leaf.1, f32[1,1,1,512,512]{4,3,2,1,0:T(8,128)} %lower_leaf.1, s32[1,1,1]{2,1,0:T(1,128)S(6)} %copy.13.present, ...), custom_call_target="tpu_custom_call" | custom-call | tf_op jit(solution)/shard_map/pallas_call | solution.py:442
  66.4 2.1 %shard_map.122 = (f32[1,1,1,512,256]{4,3,2,1,0:T(8,128)}, f32[1,1,128,256]{3,2,1,0:T(8,128)}, f32[2,128,256]{2,1,0:T(8,128)}) custom-call(f32[1,1,1,512,256]{4,3,2,1,0:T(8,128)} %get-tuple-element.6.refs_0_, f32[1,1,128,256]{3,2,1,0:T(8,128)} %get-tuple-element.7.refs_1_, f32[2,128,256]{2,1,0:T(8,128)} %get-tuple-element.8.refs_2_), custom_call_target="tpu_custom_call" | custom-call | tf_op jit(solution)/shard_map/pallas_call | solution.py:456

commit v4 on v3

--- a/solution.py
+++ b/solution.py
@@ -215,6 +215,7 @@
         split_tops()
 
     def narrow(value, m, dims):
+        rows = value.shape[0]
         rest = value - value.astype(jnp.bfloat16).astype(jnp.float32)
         both = jnp.concatenate([value, rest], axis=0).astype(jnp.bfloat16)
         high, low = s["top_high"][m], s["top_low"][m]
@@ -223,7 +224,7 @@
             return lax.dot_general(a, b, (dims, ((), ())), preferred_element_type=jnp.float32)
 
         wide = dot(both, high)
-        return wide[:chunk] + (wide[chunk:] + dot(both, low)[:chunk])
+        return wide[:rows] + (wide[rows:] + dot(both, low)[:rows])
 
     def index(known, bit=None, flip=False):
         where = []
@@ -265,22 +266,46 @@
             for copy in copies:
                 copy.wait()
 
+    own = index(plan.halved)
+
+    def solve_tops():
+        once("tops", finish_tops)
+        top_fwd = []
+        for level in range(levels):
+            residual = jnp.concatenate(
+                [s[f"top{p}_{level}"][own] for p in range(plan.parts)], axis=0
+            )
+            for lower in range(level):
+                m = levels + pair_index(level, lower)
+                residual = residual - narrow(top_fwd[lower], m, NN)
+            top_fwd.append(narrow(residual, level, NT))
+        top_back = [None] * levels
+        for level in reversed(range(levels)):
+            residual = top_fwd[level]
+            for higher in range(level + 1, levels):
+                m = levels + pair_index(higher, level)
+                residual = residual - narrow(top_back[higher], m, NT)
+            top_back[level] = narrow(residual, level, NN)
+            for p in range(plan.parts):
+                s[f"back{p}_{level}"][own] = top_back[level][p * chunk : (p + 1) * chunk]
+
     def pipeline(p):
         cols = slice(p * width, (p + 1) * width)
-        own = index(plan.halved)
+        last = p == plan.parts - 1
         mid, mid_full = s["mid"].at[p], s["mid_full"].at[p]
         part = mul(lower_pair, split(s["leaf_fwd"][:, cols])) * kept
         mid[...] = part.reshape(n, share, width)
         for t, _ in enumerate(scatter_sum(mid, s["mid_land"].at[p])):
-            if t == nbits - 1:
-                once("middle", fill_middle)
-                once("lower", fill_lower)
+            if t == nbits - 1 and last:
+                fill_middle()
+                fill_lower()
             yield
         mid_full[me] = right_middle[0, 0, :, cols] - mid[me]
         for t, _ in enumerate(gather(mid_full)):
             if t == 0:
                 once("over", send_over)
-                once("inverse", fill_inverse)
+                if last:
+                    fill_inverse()
             yield
         once("up", send_up)
         middle_fwd = mul(kept_pair("im"), split(mid_full[...].reshape(block, width)))
@@ -321,36 +346,24 @@
                 )
                 for level in range(levels)
             ]
-            once("tops", finish_tops)
+            if last:
+                once("tops", finish_tops)
             yield
             for level in range(levels):
                 top = s[f"top{p}_{level}"]
                 copies[level].wait()
                 top[own] = top[own] + s[f"rest{p}"][step, level]
 
-        once("tops", finish_tops)
-        top_fwd = []
-        for level in range(levels):
-            residual = s[f"top{p}_{level}"][own]
-            for lower in range(level):
-                m = levels + pair_index(level, lower)
-                residual = residual - narrow(top_fwd[lower], m, NN)
-            top_fwd.append(narrow(residual, level, NT))
-        top_back = [None] * levels
-        for level in reversed(range(levels)):
-            residual = top_fwd[level]
-            for higher in range(level + 1, levels):
-                m = levels + pair_index(higher, level)
-                residual = residual - narrow(top_back[higher], m, NT)
-            top_back[level] = narrow(residual, level, NN)
-            s[f"back{p}_{level}"][own] = top_back[level]
+        yield
+        once("solve", solve_tops)
         for step in reversed(range(len(plan.halved))):
             copies = []
             for level in range(levels):
                 order = plan.order(level)
                 held = s[f"back{p}_{level}"].at[index(order[: step + 1])]
                 copies.append(ship(held, held, partner(order[step])))
-            once("turned", fill_middle_turned)
+            if last:
+                once("turned", fill_middle_turned)
             yield
             for copy in copies:
                 copy.wait()
@@ -361,17 +374,17 @@
             residual = residual - mul(kept_pair("um", level), split(turned), NT)
         mid2, mid2_full = s["mid2"].at[p], s["mid2_full"].at[p]
         mid2[...] = mul(kept_pair("imt"), split(residual)).reshape(n, share, width)
-        steps = scatter_sum(mid2, s["mid2_land"].at[p])
+        yield from scatter_sum(mid2, s["mid2_land"].at[p])
+        mid2_full[me] = mid2[me]
+        steps = gather(mid2_full)
         next(steps)
+        solve_middle[0, 0, :, cols] = mid2[me]
         for level in range(levels):
             rows = s["top_rows"].at[level]
             rows[...] = s[f"back{p}_{level}"][...].reshape(width, block).T
             solve_top[level, :, cols] = rows[pl.ds(pl.multiple_of(me * share, share), share), :]
         yield
         yield from steps
-        solve_middle[0, 0, :, cols] = mid2[me]
-        mid2_full[me] = mid2[me]
-        yield from gather(mid2_full)
         middle = split(mid2_full[...].reshape(block, width))
         leaf_res = s["leaf_fwd"][:, cols] - kept * mul(
             (s["low_high"][...], s["low_low"][...]), middle

time: 68.7 us -> 69 us (level)
  no operation moved by 1% of the time
where the time goes in v4:
time: 69 us; the launch traced here: 68.9 us
  Pallas kernels  67.6 us (98%)
  between operations  1.29 us (2%)
    pallas_call x1, Pallas kernels, local(): pl.pallas_call(functools.partial(kernel, plan), out_shape=(jax.ShapeDtype...  65.5 us
    pallas_call x1, Pallas kernels, local(): pl.pallas_call(copy_out, out_shape=tuple((jax.ShapeDtypeStruct(x.shape, x...  2.11 us

profile of v4, /device:TPU:0, one launch (start us, length us, event | category | flops | bytes accessed | tf_op | source)
XLA Modules:
  0.0 68.9 jit_solution(10009973663971147844)
XLA Ops:
  1.3 65.5 %shard_map.121 = (f32[1,1,1,512,256]{4,3,2,1,0:T(8,128)}, f32[1,1,128,256]{3,2,1,0:T(8,128)}, f32[2,128,256]{2,1,0:T(8,128)}) custom-call(f32[1,1,1,512,256]{4,3,2,1,0:T(8,128)} %right_leaf.1, f32[1,1,1,512,512]{4,3,2,1,0:T(8,128)} %inverse_leaf.1, f32[1,1,1,512,512]{4,3,2,1,0:T(8,128)} %lower_leaf.1, s32[1,1,1]{2,1,0:T(1,128)S(6)} %copy.13.present, ...), custom_call_target="tpu_custom_call" | custom-call | tf_op jit(solution)/shard_map/pallas_call | solution.py:455
  66.8 2.1 %shard_map.122 = (f32[1,1,1,512,256]{4,3,2,1,0:T(8,128)}, f32[1,1,128,256]{3,2,1,0:T(8,128)}, f32[2,128,256]{2,1,0:T(8,128)}) custom-call(f32[1,1,1,512,256]{4,3,2,1,0:T(8,128)} %get-tuple-element.6.refs_0_, f32[1,1,128,256]{3,2,1,0:T(8,128)} %get-tuple-element.7.refs_1_, f32[2,128,256]{2,1,0:T(8,128)} %get-tuple-element.8.refs_2_), custom_call_target="tpu_custom_call" | custom-call | tf_op jit(solution)/shard_map/pallas_call | solution.py:469
